TPU v7x, 128 devices: a whole 4x4x4 slice. The times are simulated.
128 devices in a mesh: blk: 32 (over x, z_hi, y), frq: 4 (over z_lo, core).
Axes of the slice: x: 4, y: 4, z: 4 (z_hi: 2, z_lo: 2; z = z_hi * 2 + z_lo), core: 2. Of those that a mesh axis runs over, the one named last changes fastest.
Arguments:
- spectra: bfloat16 [2, 4096, 64, 512], P(None, 'blk', None, 'frq'), may hold values from -6 to 6
- live: int32 [4096], P('blk'), may hold values 0 or 1
Outputs:
- xcorr: float32 [3, 4096, 128, 128], P(None, ('blk', 'frq'))
All inputs are finite; a program needn't handle non-finite values. No bound on the sum of `live` on one device may be relied on, other than what follows from the above.
Results may differ from a plain program's by a relative error of at most 0.0058.
Values may be sent and summed in bfloat16 or wider, within the bound.
A program may use at most 128 MiB of HBM per device.

v0:
```python
import math

import jax
import jax.numpy as jnp
from jax import lax
from jax.sharding import PartitionSpec as P

F = 512
W = 64
LAGS = 128
ROUNDS = 3


EPSILON = 1e-06


def shifted(shard, axis, by):
    length = lax.axis_size(axis)
    return lax.ppermute(shard, axis, [(i, (i + by) % length) for i in range(length)])


def normalize(spectra, live):
    values = spectra.astype(jnp.float32)
    energy = jnp.mean(values * values, axis=(0, 2), keepdims=True)
    weight = live.astype(jnp.float32)[None, :, None, None] * lax.rsqrt(energy + EPSILON)
    return (values * weight).astype(jnp.bfloat16)


def lag_table(first_bin, bin_count, length_all, lag_count):
    bins = first_bin + jnp.arange(bin_count, dtype=jnp.int32)
    delays = jnp.arange(lag_count, dtype=jnp.int32) - lag_count // 2
    residue = jnp.mod(bins[:, None] * delays[None, :], 2 * length_all)
    phases = residue.astype(jnp.float32) * (math.pi / length_all)
    factor = 1.0 / math.sqrt(length_all)
    return jnp.stack([jnp.cos(phases) * factor, -jnp.sin(phases) * factor], 0).astype(jnp.bfloat16)


def cross_block(local_block, remote_block):

    def product(left, right):
        return jnp.einsum("cwf,dwf->cdf", left, right, preferred_element_type=jnp.float32)

    factor = 1.0 / math.sqrt(W)
    real_part = (
        product(local_block[0], remote_block[0]) + product(local_block[1], remote_block[1])
    ) * factor
    imag_part = (
        product(local_block[1], remote_block[0]) - product(local_block[0], remote_block[1])
    ) * factor
    return jnp.stack([real_part, imag_part], axis=2).astype(jnp.bfloat16)


def local(spectra, live):
    normed = normalize(spectra, live)
    local_bins = spectra.shape[3]
    rows_here = spectra.shape[1] // lax.axis_size("frq")
    used_table = lag_table(lax.axis_index("frq") * local_bins, local_bins, F, LAGS)
    outputs = []
    partner = normed
    for offset in range(1, ROUNDS + 1):
        partner = shifted(partner, "blk", -1)
        cross_spec = cross_block(normed, partner)

        def partial_time(first_row, row_count, source=cross_spec):
            return jnp.einsum(
                "cdpf,pfl->cdl", source, used_table, preferred_element_type=jnp.float32
            )

        lagged = lax.psum_scatter(
            partial_time(jnp.int32(0), rows_here * lax.axis_size("frq")),
            "frq",
            scatter_dimension=0,
            tiled=True,
        )
        outputs.append(lagged)
    return jnp.stack(outputs, 0)


def solution(mesh):
    return jax.shard_map(
        local,
        mesh=mesh,
        in_specs=(P(None, "blk", None, "frq"), P("blk")),
        out_specs=P(None, ("blk", "frq"), None, None),
        check_vma=False,
    )
```

profile of v0, /device:TPU:1, one launch (start us, length us, event | category | flops | bytes accessed | tf_op | source)
XLA Modules:
  0.0 599.7 jit_solution(15285767817980559662)
XLA Ops:
  6.5 0.0 reduce-scatter.4.cloned.1.call-start
  6.5 7.3 %copy.3 = bf16[2,128,64,128]{1,2,3,0:T(8,128)(2,1)} copy(bf16[2,128,64,128]{3,2,1,0:T(8,128)(2,1)} %param.2) | data formatting | bytes 8388608 | tf_op args[0]
  13.8 0.0 copy-start.3
  13.8 0.0 copy-start
  13.8 3.5 fusion
  17.4 0.0 copy-done.3
  17.4 0.0 copy-done
  17.5 3.2 fusion.1
  20.6 9.1 %collective-permute-start = (bf16[2,128,64,128]{1,2,3,0:T(8,128)(2,1)}, bf16[2,128,64,128]{1,2,3,0:T(8,128)(2,1)}, u32[]{:S(2)}, u32[]{:S(2)}) collective-permute-start(bf16[2,128,64,128]{1,2,3,0:T(8,128)(2,1)} %fusion.1), channel_id=1, source_target_pairs={{0,124},{4,0},{8,4},{12,8},{16,12},{20,16},{24,20},{28,24},{32,28}... | collective-permute-start | bytes 12582920 | tf_op jit(solution)/shard_map/ppermute | solution.py:19
  29.7 0.4 multiply_convert_fusion.7
  30.1 89.2 %collective-permute-done = bf16[2,128,64,128]{1,2,3,0:T(8,128)(2,1)} collective-permute-done((bf16[2,128,64,128]{1,2,3,0:T(8,128)(2,1)}, bf16[2,128,64,128]{1,2,3,0:T(8,128)(2,1)}, u32[]{:S(2)}, u32[]{:S(2)}) %collective-permute-start) | collective-permute-done | bytes 4194336 | tf_op jit(solution)/shard_map/ppermute | solution.py:19
  119.3 3.5 fusion.9
  122.8 3.6 fusion.8
  126.4 4.0 fusion.2
  130.4 6.0 %fusion.3 = bf16[128,128,1,128]{0,1,3,2:T(8,128)(2,1)} fusion(f32[128,128,128]{2,1,0:T(8,128)S(1)} %fusion.8, bf16[2,128,64,128]{1,2,3,0:T(8,128)(2,1)} %collective-permute-done, bf16[2,128,64,128]{1,2,3,0:T(8,128)(2,1)} %fusion.1), kind=kOutput, calls=%fused_computation.15 | convolution fusion | flops 274726912 | bytes 16777216 | tf_op jit(solution)/shard_map/cwf,dwf->cdf/dot_general | solution.py:41
  136.5 6.2 %pad_maximum_fusion = bf16[128,128,2,128]{0,1,3,2:T(8,128)(2,1)} fusion(bf16[128,128,1,128]{0,1,3,2:T(8,128)(2,1)} %fusion.3, bf16[128,128,1,128]{0,1,3,2:T(8,128)(2,1)S(1)} %fusion.2), kind=kLoop, calls=%fused_computation.4 | loop fusion | flops 4194304 | bytes 16777216 | tf_op jit(solution)/shard_map/stack | solution.py:50
  142.6 13.5 %copy.4 = bf16[128,128,2,128]{3,1,2,0:T(8,128)(2,1)} copy(bf16[128,128,2,128]{0,1,3,2:T(8,128)(2,1)} %pad_maximum_fusion) | data formatting | bytes 16777216 | tf_op jit(solution)/shard_map/stack | solution.py:50
  156.2 8.9 %convolution_bitcast_fusion.2 = f32[128,128,128]{2,1,0:T(8,128)} fusion(bf16[128,128,2,128]{3,1,2,0:T(8,128)(2,1)} %copy.4, bf16[1,128,128]{2,1,0:T(8,128)(2,1)S(1)} %get-tuple-element.6, bf16[1,128,128]{2,1,0:T(8,128)(2,1)S(1)} %get-tuple-element.5), kind=kOutput, calls=%fused_computation.22 | convolution fusion | flops 1073774592 | bytes 16842752 | tf_op jit(solution)/shard_map/cdpf,pfl->cdl/dot_general | solution.py:65
  165.1 0.0 reduce-scatter.4.cloned.1.call-update
  165.2 0.0 reduce-scatter.6.cloned.1.call-start
  165.2 8.2 %collective-permute-start.1 = (bf16[2,128,64,128]{1,2,3,0:T(8,128)(2,1)}, bf16[2,128,64,128]{1,2,3,0:T(8,128)(2,1)S(1)}, u32[]{:S(2)}, u32[]{:S(2)}) collective-permute-start(bf16[2,128,64,128]{1,2,3,0:T(8,128)(2,1)} %collective-permute-done), channel_id=1, source_target_pairs={{0,124},{4,0},{8,4},{12,8},{16,12},{20,16},{24,20},{28,24},{32,28}... | collective-permute-start | bytes 12582920 | tf_op jit(solution)/shard_map/ppermute | solution.py:19
  173.4 88.6 %collective-permute-done.1 = bf16[2,128,64,128]{1,2,3,0:T(8,128)(2,1)S(1)} collective-permute-done((bf16[2,128,64,128]{1,2,3,0:T(8,128)(2,1)}, bf16[2,128,64,128]{1,2,3,0:T(8,128)(2,1)S(1)}, u32[]{:S(2)}, u32[]{:S(2)}) %collective-permute-start.1) | collective-permute-done | bytes 4194336 | tf_op jit(solution)/shard_map/ppermute | solution.py:19
  262.0 4.4 fusion.11
  266.5 0.0 copy-done.1
  266.5 2.9 fusion.10
  269.4 4.1 fusion.4
  273.5 6.0 %fusion.5 = bf16[128,128,1,128]{0,1,3,2:T(8,128)(2,1)} fusion(f32[128,128,128]{2,1,0:T(8,128)S(1)} %fusion.10, bf16[2,128,64,128]{1,2,3,0:T(8,128)(2,1)} %copy-done.1, bf16[2,128,64,128]{1,2,3,0:T(8,128)(2,1)} %fusion.1), kind=kOutput, calls=%fused_computation.17 | convolution fusion | flops 274726912 | bytes 16777216 | tf_op jit(solution)/shard_map/cwf,dwf->cdf/dot_general | solution.py:41
  279.5 6.2 %pad_maximum_fusion.1 = bf16[128,128,2,128]{0,1,3,2:T(8,128)(2,1)} fusion(bf16[128,128,1,128]{0,1,3,2:T(8,128)(2,1)} %fusion.5, bf16[128,128,1,128]{0,1,3,2:T(8,128)(2,1)S(1)} %fusion.4), kind=kLoop, calls=%fused_computation.5 | loop fusion | flops 4194304 | bytes 16777216 | tf_op jit(solution)/shard_map/stack | solution.py:50
  285.7 13.5 %copy.5 = bf16[128,128,2,128]{3,1,2,0:T(8,128)(2,1)} copy(bf16[128,128,2,128]{0,1,3,2:T(8,128)(2,1)} %pad_maximum_fusion.1) | data formatting | bytes 16777216 | tf_op jit(solution)/shard_map/stack | solution.py:50
  299.2 8.9 %convolution_bitcast_fusion.1 = f32[128,128,128]{2,1,0:T(8,128)} fusion(bf16[128,128,2,128]{3,1,2,0:T(8,128)(2,1)} %copy.5, bf16[1,128,128]{2,1,0:T(8,128)(2,1)S(1)} %get-tuple-element.6, bf16[1,128,128]{2,1,0:T(8,128)(2,1)S(1)} %get-tuple-element.5), kind=kOutput, calls=%fused_computation.21 | convolution fusion | flops 1073774592 | bytes 16842752 | tf_op jit(solution)/shard_map/cdpf,pfl->cdl/dot_general | solution.py:65
  308.2 0.0 reduce-scatter.6.cloned.1.call-update
  308.2 0.0 reduce-scatter.8.cloned.1.call-start
  308.2 8.5 %collective-permute-start.2 = (bf16[2,128,64,128]{1,2,3,0:T(8,128)(2,1)}, bf16[2,128,64,128]{1,2,3,0:T(8,128)(2,1)S(1)}, u32[]{:S(2)}, u32[]{:S(2)}) collective-permute-start(bf16[2,128,64,128]{1,2,3,0:T(8,128)(2,1)} %copy-done.1), channel_id=1, source_target_pairs={{0,124},{4,0},{8,4},{12,8},{16,12},{20,16},{24,20},{28,24},{32,28}... | collective-permute-start | bytes 12582920 | tf_op jit(solution)/shard_map/ppermute | solution.py:19
  316.7 87.7 %collective-permute-done.2 = bf16[2,128,64,128]{1,2,3,0:T(8,128)(2,1)S(1)} collective-permute-done((bf16[2,128,64,128]{1,2,3,0:T(8,128)(2,1)}, bf16[2,128,64,128]{1,2,3,0:T(8,128)(2,1)S(1)}, u32[]{:S(2)}, u32[]{:S(2)}) %collective-permute-start.2) | collective-permute-done | bytes 4194336 | tf_op jit(solution)/shard_map/ppermute | solution.py:19
  404.4 0.0 copy-start.2
  404.4 4.4 fusion.13
  408.8 0.0 copy-done.2
  408.8 2.9 fusion.12
  411.8 4.0 fusion.6
  415.8 6.0 %fusion.7 = bf16[128,128,1,128]{0,1,3,2:T(8,128)(2,1)} fusion(f32[128,128,128]{2,1,0:T(8,128)S(1)} %fusion.12, bf16[2,128,64,128]{1,2,3,0:T(8,128)(2,1)} %copy-done.2, bf16[2,128,64,128]{1,2,3,0:T(8,128)(2,1)} %fusion.1), kind=kOutput, calls=%fused_computation.19 | convolution fusion | flops 274726912 | bytes 16777216 | tf_op jit(solution)/shard_map/cwf,dwf->cdf/dot_general | solution.py:41
  421.9 6.2 %pad_maximum_fusion.2 = bf16[128,128,2,128]{0,1,3,2:T(8,128)(2,1)} fusion(bf16[128,128,1,128]{0,1,3,2:T(8,128)(2,1)} %fusion.7, bf16[128,128,1,128]{0,1,3,2:T(8,128)(2,1)S(1)} %fusion.6), kind=kLoop, calls=%fused_computation.6 | loop fusion | flops 4194304 | bytes 16777216 | tf_op jit(solution)/shard_map/stack | solution.py:50
  428.0 13.5 %copy.6 = bf16[128,128,2,128]{3,1,2,0:T(8,128)(2,1)} copy(bf16[128,128,2,128]{0,1,3,2:T(8,128)(2,1)} %pad_maximum_fusion.2) | data formatting | bytes 16777216 | tf_op jit(solution)/shard_map/stack | solution.py:50
  441.6 9.0 %convolution_bitcast_fusion = f32[128,128,128]{2,1,0:T(8,128)} fusion(bf16[128,128,2,128]{3,1,2,0:T(8,128)(2,1)} %copy.6, bf16[1,128,128]{2,1,0:T(8,128)(2,1)S(1)} %get-tuple-element.6, bf16[1,128,128]{2,1,0:T(8,128)(2,1)S(1)} %get-tuple-element.5), kind=kOutput, calls=%fused_computation.20 | convolution fusion | flops 1073774592 | bytes 16842752 | tf_op jit(solution)/shard_map/cdpf,pfl->cdl/dot_general | solution.py:65
  450.6 0.0 reduce-scatter.8.cloned.1.call-update
  450.6 0.0 reduce-scatter.4.cloned.1.call-done
  450.7 53.5 %reduce-scatter.6.cloned.1.call-done = f32[32,128,128]{2,1,0:T(8,128)} async-done(((f32[128,128,128]{2,1,0:T(8,128)}), f32[32,128,128]{2,1,0:T(8,128)}) %reduce-scatter.6.cloned.1.call-update) | async-done | bytes 2097168 | tf_op jit(solution)/shard_map/reduce_scatter | solution.py:69
  504.2 82.6 %reduce-scatter.8.cloned.1.call-done = f32[32,128,128]{2,1,0:T(8,128)} async-done(((f32[128,128,128]{2,1,0:T(8,128)}), f32[32,128,128]{2,1,0:T(8,128)}) %reduce-scatter.8.cloned.1.call-update) | async-done | bytes 2097168 | tf_op jit(solution)/shard_map/reduce_scatter | solution.py:69
  586.8 6.4 %pad_maximum_fusion.3 = f32[3,32,128,128]{3,2,1,0:T(8,128)} fusion(f32[1,32,128,128]{3,2,1,0:T(8,128)} %bitcast.86, f32[1,32,128,128]{3,2,1,0:T(8,128)} %bitcast.85, f32[1,32,128,128]{3,2,1,0:T(8,128)} %bitcast.84), kind=kLoop, calls=%fused_computation.13 | loop fusion | flops 3145728 | bytes 12582912 | tf_op jit(solution)/shard_map/stack | solution.py:76
  (4 shorter events, 0.0 us)
Async XLA Ops:
  6.5 444.1 %reduce-scatter.4.cloned.1.call-start = ((), (), s32[]{:S(2)}) async-start(), calls=%async_computation.3 | async-start | bytes 10485760 | tf_op jit(solution)/shard_map/reduce_scatter | solution.py:69
  13.8 3.6 copy-start.3
  13.8 3.6 copy-start
  20.6 98.6 %collective-permute-start = (bf16[2,128,64,128]{1,2,3,0:T(8,128)(2,1)}, bf16[2,128,64,128]{1,2,3,0:T(8,128)(2,1)}, u32[]{:S(2)}, u32[]{:S(2)}) collective-permute-start(bf16[2,128,64,128]{1,2,3,0:T(8,128)(2,1)} %fusion.1), channel_id=1, source_target_pairs={{0,124},{4,0},{8,4},{12,8},{16,12},{20,16},{24,20},{28,24},{32,28}... | collective-permute-start | bytes 12582920 | tf_op jit(solution)/shard_map/ppermute | solution.py:19
  165.2 339.0 %reduce-scatter.6.cloned.1.call-start = ((), (), s32[]{:S(2)}) async-start(), calls=%async_computation.4 | async-start | bytes 10485760 | tf_op jit(solution)/shard_map/reduce_scatter | solution.py:69
  165.2 96.8 %collective-permute-start.1 = (bf16[2,128,64,128]{1,2,3,0:T(8,128)(2,1)}, bf16[2,128,64,128]{1,2,3,0:T(8,128)(2,1)S(1)}, u32[]{:S(2)}, u32[]{:S(2)}) collective-permute-start(bf16[2,128,64,128]{1,2,3,0:T(8,128)(2,1)} %collective-permute-done), channel_id=1, source_target_pairs={{0,124},{4,0},{8,4},{12,8},{16,12},{20,16},{24,20},{28,24},{32,28}... | collective-permute-start | bytes 12582920 | tf_op jit(solution)/shard_map/ppermute | solution.py:19
  262.0 4.5 copy-start.1
  308.2 278.6 %reduce-scatter.8.cloned.1.call-start = ((), (), s32[]{:S(2)}) async-start(), calls=%async_computation.5 | async-start | bytes 10485760 | tf_op jit(solution)/shard_map/reduce_scatter | solution.py:69
  308.2 96.1 %collective-permute-start.2 = (bf16[2,128,64,128]{1,2,3,0:T(8,128)(2,1)}, bf16[2,128,64,128]{1,2,3,0:T(8,128)(2,1)S(1)}, u32[]{:S(2)}, u32[]{:S(2)}) collective-permute-start(bf16[2,128,64,128]{1,2,3,0:T(8,128)(2,1)} %copy-done.1), channel_id=1, source_target_pairs={{0,124},{4,0},{8,4},{12,8},{16,12},{20,16},{24,20},{28,24},{32,28}... | collective-permute-start | bytes 12582920 | tf_op jit(solution)/shard_map/ppermute | solution.py:19
  404.4 4.5 copy-start.2
Sparse Core Ops, SparseCore 0:
  165.3 81.9 reduce-scatter.3
  308.3 195.8 reduce-scatter.5
  506.7 80.0 reduce-scatter.7
where the time goes:
time: 601 us; the launch traced here: 600 us
  waiting for transfers between devices  402 us (67%)
  matrix products  79 us (13%)
  local copies, waits for them, and re-layouts  47.9 us (8%)
  other arithmetic  32 us (5%)
  starting transfers between devices  25.8 us (4%)
  between operations  13.2 us (2%)
    ppermute x3, waiting for transfers between devices, shifted(): lax.ppermute(shard, axis, [(i, (i + by) % length) for i in range(length)])  265 us
    reduce_scatter x3, waiting for transfers between devices, local(): lax.psum_scatter(partial_time(jnp.int32(0), rows_here * lax.axis_size('fr...  136 us
    dot_general x12, matrix products, product(): jnp.einsum('cwf,dwf->cdf', left, right, preferred_element_type=jnp.float32)  52.1 us
    another operation x3, local copies, waits for them, and re-layouts, cross_block(): return jnp.stack([real_part, imag_part], axis=2).astype(jnp.bfloat16)  40.6 us
    dot_general x3, matrix products, partial_time(): jnp.einsum('cdpf,pfl->cdl', source, used_table, preferred_element_type=jn...  26.9 us
    ppermute x3, starting transfers between devices, shifted(): lax.ppermute(shard, axis, [(i, (i + by) % length) for i in range(length)])  25.8 us
    another operation x3, other arithmetic, cross_block(): return jnp.stack([real_part, imag_part], axis=2).astype(jnp.bfloat16)  18.5 us
  transfers between devices with their start and end apart: 6, of which 5 were waited for; matrix products, arithmetic and copies ran while one was open for 15% of the time, Pallas kernels for 0%

commit v1 on v0

v1 whole, which is shorter than its diff:
```python
import math

import jax
import jax.numpy as jnp
from jax import lax
from jax.experimental import pallas as pl
from jax.experimental.pallas import tpu as pltpu
from jax.sharding import PartitionSpec as P

F = 512
W = 64
LAGS = 128
ROUNDS = 3
BLOCK = 128
EPSILON = 1e-06

N_BLK = 32
RING = 4
CHUNKS = 4
ROWS = 32
BINS = 128
DEPTH = 128

F_UNROLL = 16
D_UNROLL = 8
C_UNROLL = 8

MESH = pl.DeviceIdType.MESH

STEPS = [
    (1, 0), (1, 1), (3, 0), (1, 2), (3, 1), (1, 3), (3, 2),
    (2, 0), (2, 1), (2, 2), (3, 3), (2, 3),
]
PASS_ON = {0: [0], 1: [1], 3: [2], 5: [3]}
SEND_SLOTS = 3
SUM_SLOTS = 4
LATE = 3


def lag_table(first_bin, bin_count, length_all, lag_count):
    bins = first_bin + jnp.arange(bin_count, dtype=jnp.int32)
    delays = jnp.arange(lag_count, dtype=jnp.int32) - lag_count // 2
    residue = jnp.mod(bins[:, None] * delays[None, :], 2 * length_all)
    phases = residue.astype(jnp.float32) * (math.pi / length_all)
    factor = 1.0 / math.sqrt(length_all)
    return jnp.stack([jnp.cos(phases) * factor, -jnp.sin(phases) * factor], 0).astype(jnp.bfloat16)


def normalize_chunk(spectra, live, turned, block, chunk):
    def channels(i, _):
        for u in range(C_UNROLL):
            row = i * C_UNROLL + u
            channel = chunk * ROWS + row
            values = spectra[:, channel].reshape(DEPTH, BINS).astype(jnp.float32)
            energy = jnp.sum(values * values, axis=0, keepdims=True) * (1.0 / DEPTH)
            weight = lax.rsqrt(energy + EPSILON) * live[channel].astype(jnp.float32)
            normed = (values * weight).astype(jnp.bfloat16).astype(jnp.float32)
            turned[pl.ds(row, BINS, stride=ROWS), :] = normed.T
        return 0

    lax.fori_loop(0, ROWS // C_UNROLL, channels, 0)

    def bins(i, _):
        for u in range(8):
            f = i * 8 + u
            rows = pl.ds(pl.multiple_of(f * ROWS, ROWS), ROWS)
            block[chunk, f] = turned[rows, :].astype(jnp.bfloat16)
        return 0

    lax.fori_loop(0, BINS // 8, bins, 0)


def cross_chunk(own, partner, cross, order):
    sign = jnp.where(lax.broadcasted_iota(jnp.int32, (ROWS, DEPTH), 1) < W, -1.0, 1.0)

    def bins(i, _):
        for u in range(F_UNROLL):
            f = i * F_UNROLL + u
            there = partner[f]
            swapped = (pltpu.roll(there.astype(jnp.float32), W, axis=1) * sign).astype(jnp.bfloat16)
            both = jnp.concatenate([there, swapped], axis=0)
            here = jnp.concatenate([own[o, f] for o in order], axis=0)
            parts = lax.dot_general(
                both, here, (((1,), (1,)), ((), ())), preferred_element_type=jnp.float32
            )
            cross[pl.ds(f, ROWS, stride=2 * BINS), :] = parts[:ROWS]
            cross[pl.ds(BINS + f, ROWS, stride=2 * BINS), :] = parts[ROWS:]
        return 0

    lax.fori_loop(0, BINS // F_UNROLL, bins, 0)


def lag_chunk(cross, table, keep, give):
    def channels(i, _):
        for u in range(D_UNROLL):
            j = i * D_UNROLL + u
            rows = pl.ds(pl.multiple_of(j * 2 * BINS, 2 * BINS), 2 * BINS)
            lags = lax.dot_general(
                cross[rows, :].astype(jnp.bfloat16),
                table[...],
                (((0,), (0,)), ((), ())),
                preferred_element_type=jnp.float32,
            )
            keep[0, j] = lags[:ROWS]
            keep[1, j] = lags[ROWS:2 * ROWS]
            give[0, j] = lags[2 * ROWS:3 * ROWS].astype(jnp.bfloat16)
            give[1, j] = lags[3 * ROWS:].astype(jnp.bfloat16)
        return 0

    lax.fori_loop(0, ROWS // D_UNROLL, channels, 0)


def kernel(
    spectra, live, table, out,
    first, second, third, passing, turned, cross, keep, total,
    core_out, core_in, pair_out, pair_in,
    down_send, up_send, far_send, second_recv, third_recv, far_recv,
    core_send, core_recv, pair_send, pair_recv,
):
    b = lax.axis_index("blk")
    q = lax.axis_index("frq")
    y = b % RING
    ring = b - y
    core = q + 1 - 2 * (q % 2)
    pair = (q + 2) % 4
    both = (core + 2) % 4
    order = [q, pair, core, both]
    below = (ring + (y + RING - 1) % RING, q)
    above = (ring + (y + 1) % RING, q)
    far_to = ((b + N_BLK - RING) % N_BLK, q)
    far_from = ((b + RING) % N_BLK, q)
    after = (b + 1) % N_BLK
    before = (b + N_BLK - 1) % N_BLK

    barrier = pltpu.get_barrier_semaphore()
    greeted = [
        below, above, far_to, far_from, (b, core), (b, pair),
        (after, q), (after, pair), (before, q), (before, pair),
    ]
    for device in greeted:
        pl.semaphore_signal(barrier, inc=1, device_id=device, device_id_type=MESH)

    def remote(src, dst, send, recv, device):
        return pltpu.make_async_remote_copy(
            src_ref=src, dst_ref=dst, send_sem=send, recv_sem=recv,
            device_id=device, device_id_type=MESH,
        )

    def down(src, c):
        return remote(src.at[c], second.at[c], down_send.at[c], second_recv.at[c], below)

    def up(src, c):
        return remote(src.at[c], third.at[c], up_send.at[c], third_recv.at[c], above)

    def far(c):
        return remote(first.at[c], passing.at[c], far_send.at[c], far_recv.at[c], far_to)

    for c in range(CHUNKS):
        normalize_chunk(spectra, live, turned, first, c)
        if c == 0:
            pl.semaphore_wait(barrier, len(greeted))

        @pl.when(y < RING - 1)
        def _():
            far(c).start()

        @pl.when(y > 0)
        def _():
            down(first, c).start()

        @pl.when(y == RING - 1)
        def _():
            up(first, c).start()

    def pass_on(c):
        @pl.when(y < RING - 1)
        def _():
            far(c).wait_recv()
            up(passing, c).start()

        @pl.when(y == 0)
        def _():
            down(passing, c).start()

    def core_copy(s):
        slot = s % SEND_SLOTS
        return remote(core_out.at[slot], core_in.at[s], core_send.at[s], core_recv.at[s], (b, core))

    def pair_copies(s):
        r, c = STEPS[s]
        slot = s % SUM_SLOTS
        if r == 2:
            a, z = 8 + c, 12 + c
            return [
                remote(pair_out.at[slot, 0], pair_in.at[a], pair_send.at[a], pair_recv.at[a], (after, q)),
                remote(pair_out.at[slot, 1], pair_in.at[z], pair_send.at[z], pair_recv.at[z], (after, pair)),
            ]
        a = (r // 2) * 4 + c
        return [remote(pair_out.at[slot, 1], pair_in.at[a], pair_send.at[a], pair_recv.at[a], (b, pair))]

    def add_cores(s):
        r, c = STEPS[s]
        core_copy(s).wait_recv()
        if s >= SUM_SLOTS:
            for copy in pair_copies(s - SUM_SLOTS):
                copy.wait_send()
        mine = keep[s % 2, 0] + core_in[s, 0].astype(jnp.float32)
        theirs = keep[s % 2, 1] + core_in[s, 1].astype(jnp.float32)
        slot = s % SUM_SLOTS
        pair_out[slot, 1] = theirs.astype(jnp.bfloat16)
        if r == 2:
            pair_out[slot, 0] = mine.astype(jnp.bfloat16)
        else:
            total[slot] = mine
        for copy in pair_copies(s):
            copy.start()

    def finish(s):
        r, c = STEPS[s]
        for copy in pair_copies(s):
            copy.wait_recv()
        if r == 2:
            lags = pair_in[8 + c].astype(jnp.float32) + pair_in[12 + c].astype(jnp.float32)
        else:
            lags = total[s % SUM_SLOTS] + pair_in[(r // 2) * 4 + c].astype(jnp.float32)
        out[r - 1, c] = lags

    for s, (r, c) in enumerate(STEPS):
        for p in PASS_ON.get(s, []):
            pass_on(p)
        if r == 1:
            down(first, c).wait_recv()
        if r == 3:
            up(first, c).wait_recv()
        here = second if r == 2 else first
        there = second if r == 1 else third
        cross_chunk(here, there.at[c], cross, order)
        if s >= SEND_SLOTS:
            core_copy(s - SEND_SLOTS).wait_send()
        lag_chunk(cross, table, keep.at[s % 2], core_out.at[s % SEND_SLOTS])
        core_copy(s).start()
        if s >= 1:
            add_cores(s - 1)
        if s >= LATE:
            finish(s - LATE)
    last = len(STEPS)
    add_cores(last - 1)
    for s in range(last - LATE, last):
        finish(s)

    for c in range(CHUNKS):
        down(first, c).wait_send()
        up(first, c).wait_send()

        @pl.when(y < RING - 1)
        def _():
            far(c).wait_send()

    for s in range(last - SEND_SLOTS, last):
        core_copy(s).wait_send()
    for s in range(last - SUM_SLOTS, last):
        for copy in pair_copies(s):
            copy.wait_send()


def local(spectra, live):
    table = lag_table(lax.axis_index("frq") * BINS, BINS, F, LAGS)
    table = (table * (1.0 / math.sqrt(W))).reshape(2 * BINS, LAGS)
    block = (CHUNKS, BINS, ROWS, DEPTH)
    piece = (ROWS, ROWS, LAGS)
    half = jnp.bfloat16
    lags = pl.pallas_call(
        kernel,
        out_shape=jax.ShapeDtypeStruct((ROUNDS, CHUNKS) + piece, jnp.float32),
        in_specs=[
            pl.BlockSpec(memory_space=pltpu.VMEM),
            pl.BlockSpec(memory_space=pltpu.SMEM),
            pl.BlockSpec(memory_space=pltpu.VMEM),
        ],
        out_specs=pl.BlockSpec(memory_space=pltpu.VMEM),
        scratch_shapes=[
            pltpu.VMEM(block, half),
            pltpu.VMEM(block, half),
            pltpu.VMEM(block, half),
            pltpu.VMEM(block, half),
            pltpu.VMEM((BINS * ROWS, DEPTH), jnp.float32),
            pltpu.VMEM((ROWS * 2 * BINS, BLOCK), jnp.float32),
            pltpu.VMEM((2, 2) + piece, jnp.float32),
            pltpu.VMEM((SUM_SLOTS,) + piece, jnp.float32),
            pltpu.VMEM((SEND_SLOTS, 2) + piece, half),
            pltpu.VMEM((len(STEPS), 2) + piece, half),
            pltpu.VMEM((SUM_SLOTS, 2) + piece, half),
            pltpu.VMEM((16,) + piece, half),
            pltpu.SemaphoreType.DMA((CHUNKS,)),
            pltpu.SemaphoreType.DMA((CHUNKS,)),
            pltpu.SemaphoreType.DMA((CHUNKS,)),
            pltpu.SemaphoreType.DMA((CHUNKS,)),
            pltpu.SemaphoreType.DMA((CHUNKS,)),
            pltpu.SemaphoreType.DMA((CHUNKS,)),
            pltpu.SemaphoreType.DMA((len(STEPS),)),
            pltpu.SemaphoreType.DMA((len(STEPS),)),
            pltpu.SemaphoreType.DMA((16,)),
            pltpu.SemaphoreType.DMA((16,)),
        ],
        compiler_params=pltpu.CompilerParams(
            collective_id=0, has_side_effects=True, vmem_limit_bytes=60 * 2**20
        ),
    )(spectra, live, table)
    return lags.reshape(ROUNDS, BLOCK, ROWS, LAGS).transpose(0, 2, 1, 3)


def solution(mesh):
    return jax.shard_map(
        local,
        mesh=mesh,
        in_specs=(P(None, "blk", None, "frq"), P("blk")),
        out_specs=P(None, ("blk", "frq"), None, None),
        check_vma=False,
    )
```

time: 601 us -> 227 us (0.38)
  the two profiles are of different devices: /device:TPU:1 before, /device:TPU:70 now
where the time goes in v1:
time: 227 us
  Pallas kernels  217 us (96%)
  local copies, waits for them, and re-layouts  9.13 us (4%)
    pallas_call x1, Pallas kernels, local(): pl.pallas_call(kernel, out_shape=jax.ShapeDtypeStruct((ROUNDS, CHUNKS) +...  217 us
    reshape x1, local copies, waits for them, and re-layouts, local(): return lags.reshape(ROUNDS, BLOCK, ROWS, LAGS).transpose(0, 2, 1, 3)  9.13 us

profile of v1, /device:TPU:70, one launch (start us, length us, event | category | flops | bytes accessed | tf_op | source)
XLA Modules:
  0.0 227.2 jit_solution(7575089902181230832)
XLA Ops:
  0.0 0.4 multiply_convert_fusion.1
  0.4 0.6 maximum_multiply_fusion
  1.0 217.1 %shard_map.28 = f32[3,4,32,32,128]{4,3,2,1,0:T(8,128)} custom-call(bf16[2,128,64,128]{3,2,1,0:T(8,128)(2,1)} %spectra.1, s32[128]{0:T(128)} %live.1, bf16[256,128]{1,0:T(8,128)(2,1)} %bitcast.6), custom_call_target="tpu_custom_call" | custom-call | tf_op jit(solution)/shard_map/pallas_call | solution.py:272
  218.1 9.1 %copy.5 = f32[3,128,32,128]{3,1,2,0:T(8,128)} copy(f32[3,128,32,128]{3,2,1,0:T(8,128)} %bitcast.5) | data formatting | bytes 12582912 | tf_op jit(solution)/shard_map/reshape | solution.py:309
  (1 shorter events, 0.0 us)

commit v2 on v1

--- a/solution.py
+++ b/solution.py
@@ -21,8 +21,8 @@
 BINS = 128
 DEPTH = 128
 
-F_UNROLL = 16
-D_UNROLL = 8
+F_UNROLL = 32
+D_UNROLL = 16
 C_UNROLL = 8
 
 MESH = pl.DeviceIdType.MESH
@@ -33,8 +33,8 @@
 ]
 PASS_ON = {0: [0], 1: [1], 3: [2], 5: [3]}
 SEND_SLOTS = 3
-SUM_SLOTS = 4
-LATE = 3
+RELEASE = 5
+FINISH = {8: [0, 1], 9: [2, 3], 10: [4, 5], 11: [6, 7]}
 
 
 def lag_table(first_bin, bin_count, length_all, lag_count):
@@ -188,7 +188,7 @@
 
     def pair_copies(s):
         r, c = STEPS[s]
-        slot = s % SUM_SLOTS
+        slot = s
         if r == 2:
             a, z = 8 + c, 12 + c
             return [
@@ -201,17 +201,15 @@
     def add_cores(s):
         r, c = STEPS[s]
         core_copy(s).wait_recv()
-        if s >= SUM_SLOTS:
-            for copy in pair_copies(s - SUM_SLOTS):
-                copy.wait_send()
         mine = keep[s % 2, 0] + core_in[s, 0].astype(jnp.float32)
         theirs = keep[s % 2, 1] + core_in[s, 1].astype(jnp.float32)
-        slot = s % SUM_SLOTS
-        pair_out[slot, 1] = theirs.astype(jnp.bfloat16)
+        pair_out[s, 1] = theirs.astype(jnp.bfloat16)
         if r == 2:
-            pair_out[slot, 0] = mine.astype(jnp.bfloat16)
+            pair_out[s, 0] = mine.astype(jnp.bfloat16)
         else:
-            total[slot] = mine
+            total[(r // 2) * 4 + c] = mine
+
+    def exchange(s):
         for copy in pair_copies(s):
             copy.start()
 
@@ -222,12 +220,15 @@
         if r == 2:
             lags = pair_in[8 + c].astype(jnp.float32) + pair_in[12 + c].astype(jnp.float32)
         else:
-            lags = total[s % SUM_SLOTS] + pair_in[(r // 2) * 4 + c].astype(jnp.float32)
+            lags = total[(r // 2) * 4 + c] + pair_in[(r // 2) * 4 + c].astype(jnp.float32)
         out[r - 1, c] = lags
 
     for s, (r, c) in enumerate(STEPS):
         for p in PASS_ON.get(s, []):
             pass_on(p)
+        if s == RELEASE:
+            for held in range(s - 1):
+                exchange(held)
         if r == 1:
             down(first, c).wait_recv()
         if r == 3:
@@ -241,11 +242,14 @@
         core_copy(s).start()
         if s >= 1:
             add_cores(s - 1)
-        if s >= LATE:
-            finish(s - LATE)
+        if s >= RELEASE:
+            exchange(s - 1)
+        for done in FINISH.get(s, []):
+            finish(done)
     last = len(STEPS)
     add_cores(last - 1)
-    for s in range(last - LATE, last):
+    exchange(last - 1)
+    for s in range(FINISH[last - 1][-1] + 1, last):
         finish(s)
 
     for c in range(CHUNKS):
@@ -258,7 +262,7 @@
 
     for s in range(last - SEND_SLOTS, last):
         core_copy(s).wait_send()
-    for s in range(last - SUM_SLOTS, last):
+    for s in range(last):
         for copy in pair_copies(s):
             copy.wait_send()
 
@@ -286,10 +290,10 @@
             pltpu.VMEM((BINS * ROWS, DEPTH), jnp.float32),
             pltpu.VMEM((ROWS * 2 * BINS, BLOCK), jnp.float32),
             pltpu.VMEM((2, 2) + piece, jnp.float32),
-            pltpu.VMEM((SUM_SLOTS,) + piece, jnp.float32),
+            pltpu.VMEM((2 * CHUNKS,) + piece, jnp.float32),
             pltpu.VMEM((SEND_SLOTS, 2) + piece, half),
             pltpu.VMEM((len(STEPS), 2) + piece, half),
-            pltpu.VMEM((SUM_SLOTS, 2) + piece, half),
+            pltpu.VMEM((len(STEPS), 2) + piece, half),
             pltpu.VMEM((16,) + piece, half),
             pltpu.SemaphoreType.DMA((CHUNKS,)),
             pltpu.SemaphoreType.DMA((CHUNKS,)),

time: 227 us -> 213 us (0.938)
  the two profiles are of different devices: /device:TPU:70 before, /device:TPU:1 now
where the time goes in v2:
time: 213 us
  Pallas kernels  203 us (95%)
  local copies, waits for them, and re-layouts  9.13 us (4%)
    pallas_call x1, Pallas kernels, local(): pl.pallas_call(kernel, out_shape=jax.ShapeDtypeStruct((ROUNDS, CHUNKS) +...  203 us
    reshape x1, local copies, waits for them, and re-layouts, local(): return lags.reshape(ROUNDS, BLOCK, ROWS, LAGS).transpose(0, 2, 1, 3)  9.13 us

profile of v2, /device:TPU:1, one launch (start us, length us, event | category | flops | bytes accessed | tf_op | source)
XLA Modules:
  0.0 213.3 jit_solution(5644040141369295762)
XLA Ops:
  0.0 0.4 multiply_convert_fusion.1
  0.4 0.6 maximum_multiply_fusion
  1.0 203.2 %shard_map.28 = f32[3,4,32,32,128]{4,3,2,1,0:T(8,128)} custom-call(bf16[2,128,64,128]{3,2,1,0:T(8,128)(2,1)} %spectra.1, s32[128]{0:T(128)} %live.1, bf16[256,128]{1,0:T(8,128)(2,1)} %bitcast.6), custom_call_target="tpu_custom_call" | custom-call | tf_op jit(solution)/shard_map/pallas_call | solution.py:276
  204.2 9.1 %copy.5 = f32[3,128,32,128]{3,1,2,0:T(8,128)} copy(f32[3,128,32,128]{3,2,1,0:T(8,128)} %bitcast.5) | data formatting | bytes 12582912 | tf_op jit(solution)/shard_map/reshape | solution.py:313
  (1 shorter events, 0.0 us)

commit v3 on v2

--- a/solution.py
+++ b/solution.py
@@ -28,9 +28,10 @@
 MESH = pl.DeviceIdType.MESH
 
 STEPS = [
-    (1, 0), (1, 1), (3, 0), (1, 2), (3, 1), (1, 3), (3, 2),
-    (2, 0), (2, 1), (2, 2), (3, 3), (2, 3),
+    (1, 0), (1, 1), (3, 0), (1, 2), (3, 1), (1, 3),
+    (2, 0), (2, 1), (3, 2), (2, 2), (3, 3), (2, 3),
 ]
+GROUPS = [[0], [1], [2], [3], [4], [5], [6, 7], [8, 9], [10, 11]]
 PASS_ON = {0: [0], 1: [1], 3: [2], 5: [3]}
 SEND_SLOTS = 3
 RELEASE = 5
@@ -70,21 +71,29 @@
     lax.fori_loop(0, BINS // 8, bins, 0)
 
 
-def cross_chunk(own, partner, cross, order):
+def cross_chunk(owns, partners, crosses, order):
     sign = jnp.where(lax.broadcasted_iota(jnp.int32, (ROWS, DEPTH), 1) < W, -1.0, 1.0)
 
     def bins(i, _):
         for u in range(F_UNROLL):
             f = i * F_UNROLL + u
-            there = partner[f]
-            swapped = (pltpu.roll(there.astype(jnp.float32), W, axis=1) * sign).astype(jnp.bfloat16)
-            both = jnp.concatenate([there, swapped], axis=0)
-            here = jnp.concatenate([own[o, f] for o in order], axis=0)
+            both = []
+            for partner in partners:
+                there = partner[f]
+                swapped = pltpu.roll(there.astype(jnp.float32), W, axis=1) * sign
+                both += [there, swapped.astype(jnp.bfloat16)]
+            here = jnp.concatenate([own[o, f] for own in owns for o in order], axis=0)
             parts = lax.dot_general(
-                both, here, (((1,), (1,)), ((), ())), preferred_element_type=jnp.float32
+                jnp.concatenate(both, axis=0),
+                here,
+                (((1,), (1,)), ((), ())),
+                preferred_element_type=jnp.float32,
             )
-            cross[pl.ds(f, ROWS, stride=2 * BINS), :] = parts[:ROWS]
-            cross[pl.ds(BINS + f, ROWS, stride=2 * BINS), :] = parts[ROWS:]
+            for k, cross in enumerate(crosses):
+                row, column = (2 * ROWS * k, 0) if len(partners) > 1 else (0, BLOCK * k)
+                columns = slice(column, column + BLOCK)
+                cross[pl.ds(f, ROWS, stride=2 * BINS), :] = parts[row:row + ROWS, columns]
+                cross[pl.ds(BINS + f, ROWS, stride=2 * BINS), :] = parts[row + ROWS:row + 2 * ROWS, columns]
         return 0
 
     lax.fori_loop(0, BINS // F_UNROLL, bins, 0)
@@ -112,7 +121,7 @@
 
 def kernel(
     spectra, live, table, out,
-    first, second, third, passing, turned, cross, keep, total,
+    first, second, third, passing, cross, cross_too, keep, total,
     core_out, core_in, pair_out, pair_in,
     down_send, up_send, far_send, second_recv, third_recv, far_recv,
     core_send, core_recv, pair_send, pair_recv,
@@ -156,7 +165,7 @@
         return remote(first.at[c], passing.at[c], far_send.at[c], far_recv.at[c], far_to)
 
     for c in range(CHUNKS):
-        normalize_chunk(spectra, live, turned, first, c)
+        normalize_chunk(spectra, live, cross, first, c)
         if c == 0:
             pl.semaphore_wait(barrier, len(greeted))
 
@@ -223,7 +232,8 @@
             lags = total[(r // 2) * 4 + c] + pair_in[(r // 2) * 4 + c].astype(jnp.float32)
         out[r - 1, c] = lags
 
-    for s, (r, c) in enumerate(STEPS):
+    def prepare(s):
+        r, c = STEPS[s]
         for p in PASS_ON.get(s, []):
             pass_on(p)
         if s == RELEASE:
@@ -233,9 +243,8 @@
             down(first, c).wait_recv()
         if r == 3:
             up(first, c).wait_recv()
-        here = second if r == 2 else first
-        there = second if r == 1 else third
-        cross_chunk(here, there.at[c], cross, order)
+
+    def after_cross(s, cross):
         if s >= SEND_SLOTS:
             core_copy(s - SEND_SLOTS).wait_send()
         lag_chunk(cross, table, keep.at[s % 2], core_out.at[s % SEND_SLOTS])
@@ -246,6 +255,23 @@
             exchange(s - 1)
         for done in FINISH.get(s, []):
             finish(done)
+
+    for group in GROUPS:
+        for s in group:
+            prepare(s)
+        owns, partners = [], []
+        for s in group:
+            r, c = STEPS[s]
+            own = (r == 2, second if r == 2 else first)
+            partner = (r == 1, c, (second if r == 1 else third).at[c])
+            if own[0] not in [o[0] for o in owns]:
+                owns.append(own)
+            if partner[:2] not in [p[:2] for p in partners]:
+                partners.append(partner)
+        crosses = [cross, cross_too][:len(group)]
+        cross_chunk([o[-1] for o in owns], [p[-1] for p in partners], crosses, order)
+        for s, done in zip(group, crosses):
+            after_cross(s, done)
     last = len(STEPS)
     add_cores(last - 1)
     exchange(last - 1)
@@ -287,7 +313,7 @@
             pltpu.VMEM(block, half),
             pltpu.VMEM(block, half),
             pltpu.VMEM(block, half),
-            pltpu.VMEM((BINS * ROWS, DEPTH), jnp.float32),
+            pltpu.VMEM((ROWS * 2 * BINS, BLOCK), jnp.float32),
             pltpu.VMEM((ROWS * 2 * BINS, BLOCK), jnp.float32),
             pltpu.VMEM((2, 2) + piece, jnp.float32),
             pltpu.VMEM((2 * CHUNKS,) + piece, jnp.float32),

time: 213 us -> 210 us (0.986)
  Pallas kernels: 203 us -> 200 us
    pallas_call x1, Pallas kernels: 203 us -> 200 us  [local(): pl.pallas_call(kernel, out_shape=jax.ShapeDtypeStruct((ROUNDS, CHUNKS) +...]
where the time goes in v3:
time: 210 us
  Pallas kernels  200 us (95%)
  local copies, waits for them, and re-layouts  9.13 us (4%)
    pallas_call x1, Pallas kernels, local(): pl.pallas_call(kernel, out_shape=jax.ShapeDtypeStruct((ROUNDS, CHUNKS) +...  200 us
    reshape x1, local copies, waits for them, and re-layouts, local(): return lags.reshape(ROUNDS, BLOCK, ROWS, LAGS).transpose(0, 2, 1, 3)  9.13 us

profile of v3, /device:TPU:1, one launch (start us, length us, event | category | flops | bytes accessed | tf_op | source)
XLA Modules:
  0.0 209.9 jit_solution(1036333723755498694)
XLA Ops:
  0.0 0.4 multiply_convert_fusion.1
  0.4 0.6 maximum_multiply_fusion
  1.0 199.8 %shard_map.28 = f32[3,4,32,32,128]{4,3,2,1,0:T(8,128)} custom-call(bf16[2,128,64,128]{3,2,1,0:T(8,128)(2,1)} %spectra.1, s32[128]{0:T(128)} %live.1, bf16[256,128]{1,0:T(8,128)(2,1)} %bitcast.6), custom_call_target="tpu_custom_call" | custom-call | tf_op jit(solution)/shard_map/pallas_call | solution.py:302
  200.8 9.1 %copy.5 = f32[3,128,32,128]{3,1,2,0:T(8,128)} copy(f32[3,128,32,128]{3,2,1,0:T(8,128)} %bitcast.5) | data formatting | bytes 12582912 | tf_op jit(solution)/shard_map/reshape | solution.py:339
  (1 shorter events, 0.0 us)

commit v4 on v3

--- a/solution.py
+++ b/solution.py
@@ -35,7 +35,7 @@
 PASS_ON = {0: [0], 1: [1], 3: [2], 5: [3]}
 SEND_SLOTS = 3
 RELEASE = 5
-FINISH = {8: [0, 1], 9: [2, 3], 10: [4, 5], 11: [6, 7]}
+FINISH = {8: [0, 1], 9: [2, 3], 10: [4, 5]}
 
 
 def lag_table(first_bin, bin_count, length_all, lag_count):
@@ -275,7 +275,7 @@
     last = len(STEPS)
     add_cores(last - 1)
     exchange(last - 1)
-    for s in range(FINISH[last - 1][-1] + 1, last):
+    for s in range(max(FINISH[max(FINISH)]) + 1, last):
         finish(s)
 
     for c in range(CHUNKS):

time: 210 us -> 210 us (level)
  no operation moved by 1% of the time
where the time goes in v4:
time: 210 us
  Pallas kernels  200 us (95%)
  local copies, waits for them, and re-layouts  9.13 us (4%)
    pallas_call x1, Pallas kernels, local(): pl.pallas_call(kernel, out_shape=jax.ShapeDtypeStruct((ROUNDS, CHUNKS) +...  200 us
    reshape x1, local copies, waits for them, and re-layouts, local(): return lags.reshape(ROUNDS, BLOCK, ROWS, LAGS).transpose(0, 2, 1, 3)  9.13 us

profile of v4, /device:TPU:1, one launch (start us, length us, event | category | flops | bytes accessed | tf_op | source)
XLA Modules:
  0.0 209.9 jit_solution(1216031919867028067)
XLA Ops:
  0.0 0.4 multiply_convert_fusion.1
  0.4 0.6 maximum_multiply_fusion
  1.0 199.8 %shard_map.28 = f32[3,4,32,32,128]{4,3,2,1,0:T(8,128)} custom-call(bf16[2,128,64,128]{3,2,1,0:T(8,128)(2,1)} %spectra.1, s32[128]{0:T(128)} %live.1, bf16[256,128]{1,0:T(8,128)(2,1)} %bitcast.6), custom_call_target="tpu_custom_call" | custom-call | tf_op jit(solution)/shard_map/pallas_call | solution.py:302
  200.8 9.1 %copy.5 = f32[3,128,32,128]{3,1,2,0:T(8,128)} copy(f32[3,128,32,128]{3,2,1,0:T(8,128)} %bitcast.5) | data formatting | bytes 12582912 | tf_op jit(solution)/shard_map/reshape | solution.py:339
  (1 shorter events, 0.0 us)
